TPU v7x, 32 devices: a whole 2x2x4 slice. The times are simulated.
32 devices in a mesh: ray: 8 (over y, x, core), tile: 4 (over z).
Axes of the slice: x: 2, y: 2, z: 4, core: 2. Of those that a mesh axis runs over, the one named last changes fastest.
Arguments:
- data: float32 [65536], P(('ray', 'tile')), may hold values from -6 to 6
- blocks: bfloat16 [8, 4, 128, 128, 128], P('ray', 'tile'), may hold values from -0.1875 to 0.1875
- block_cols: int32 [8, 4, 128], P('ray', 'tile'), may hold values from 0 to 255, as said below
- block_rows: int32 [8, 4, 128], P('ray', 'tile'), may hold values from 0 to 63
- block_counts: int32 [8, 4], P('ray', 'tile'), may hold values from 1 to 128, as said below
- reg_weight: float32 [16, 64, 128], P('tile', 'ray'), may hold values from 0.05 to 0.5
Outputs:
- model: float32 [16, 64, 128], P('tile', 'ray')
- ray_vector: float32 [65536], P(('ray', 'tile'))
Inputs may be any that keep to these rules, and one draw needn't show every extreme that they name: `block_counts`: some ray group has exactly 128 live blocks in some tile in every draw. `block_cols`: column c of a tile lies in the cells of ray index (c % 64) // 8. Of the 128 slots of one ray group in one tile, live or not, at most 32 name columns of one ray index, and in every draw 128 // 32 ray indices are named by exactly 32 slots.
All inputs are finite; a program needn't handle non-finite values.
Results may differ from a plain program's by a relative error of at most 0.0043.
Values may be sent and summed in bfloat16 or wider, within the bound.
A program may use at most 64 MiB of HBM per device.

v0:
```python
import jax
import jax.numpy as jnp
from jax import lax
from jax.sharding import PartitionSpec as P

ITERS = 2


eps = 1e-06


def padded_2(cells, sides, width):
    for axis, dim in sides:
        count = lax.axis_size(axis)
        ends = count - 1
        head = lax.slice_in_dim(cells, 0, width, axis=dim)
        tail = lax.slice_in_dim(cells, cells.shape[dim] - width, cells.shape[dim], axis=dim)
        cells = jnp.concatenate(
            [
                lax.ppermute(tail, axis, [(i, (i + 1) % count) for i in range(ends)]),
                cells,
                lax.ppermute(head, axis, [((i + 1) % count, i) for i in range(ends)]),
            ],
            axis=dim,
        )
    return cells


def laplace(field):
    padded = padded_2(field, (("ray", 1), ("tile", 0)), 1)
    padded = jnp.pad(padded, ((0, 0), (0, 0), (1, 1)))
    beside = padded[2:, 1:-1, 1:-1] + padded[:-2, 1:-1, 1:-1]
    beside = beside + padded[1:-1, 2:, 1:-1] + padded[1:-1, :-2, 1:-1]
    beside = beside + padded[1:-1, 1:-1, 2:] + padded[1:-1, 1:-1, :-2]
    return 6.0 * field - beside


def shards(data, blocks, block_cols, block_rows, block_counts, reg_weight):
    values = blocks[0, 0]
    cols = block_cols[0, 0]
    rows = block_rows[0, 0]
    count = block_counts[0, 0]
    slots = values.shape[0]
    ray_width = values.shape[1]
    depth = values.shape[2]
    size_x, size_y = (reg_weight.shape[0], reg_weight.shape[1])
    ray_count = lax.axis_size("ray")
    grid_y = size_y * ray_count
    tile_cols = size_x * grid_y
    share = data.shape[0]
    group_rays = share * lax.axis_size("tile")
    row_blocks = group_rays // ray_width
    live = (jnp.arange(slots) < count)[:, None]
    raw_rays = data
    u_rays = data
    raw_cells = jnp.zeros_like(reg_weight)
    u_cells = raw_cells
    v_prev = jnp.zeros_like(reg_weight)
    alpha_prev = jnp.float32(0.0)
    for section in range(ITERS + 1):
        if section > 0:
            whole = lax.all_gather(v_prev.astype(jnp.bfloat16), "ray", axis=1, tiled=True).reshape(
                tile_cols, depth
            )
            product = jnp.einsum(
                "brc,bc->br", values, whole[cols], preferred_element_type=jnp.float32
            )
            product = jnp.where(live, product, 0.0)
            summed = jax.ops.segment_sum(product, rows, num_segments=row_blocks)
            contribution = summed.reshape(-1)
            total_rays = lax.psum_scatter(contribution, "tile", scatter_dimension=0, tiled=True)
            raw_rays = total_rays - alpha_prev * u_rays
            raw_cells = reg_weight * laplace(v_prev) - alpha_prev * u_cells
        rays_half = lax.all_gather(raw_rays.astype(jnp.bfloat16), "tile", axis=0, tiled=True)
        squares = jnp.sum(raw_rays * raw_rays) + jnp.sum(raw_cells * raw_cells)
        transpose_grouped = rays_half.reshape(row_blocks, ray_width)
        contrib = jnp.einsum(
            "brc,br->bc", values, transpose_grouped[rows], preferred_element_type=jnp.float32
        )
        partial_value = jax.ops.segment_sum(
            jnp.where(live, contrib, 0.0), cols, num_segments=tile_cols
        )
        z_field = lax.psum_scatter(
            partial_value.reshape(size_x, grid_y, depth), "ray", scatter_dimension=1, tiled=True
        ) + laplace(reg_weight * raw_cells)
        beta = jnp.sqrt(lax.psum(squares, ("ray", "tile")) + eps)
        v_raw = z_field / beta - beta * v_prev
        alpha = jnp.sqrt(lax.psum(jnp.sum(v_raw * v_raw), ("ray", "tile")) + eps)
        u_rays = raw_rays / beta
        u_cells = raw_cells / beta
        v_now = v_raw / alpha
        if section == 0:
            w_dir = v_now
            phibar = beta
            rhobar = alpha
            model = jnp.zeros_like(reg_weight)
        else:
            rho = jnp.sqrt(rhobar * rhobar + beta * beta)
            cosine = rhobar / rho
            sine = beta / rho
            theta = sine * alpha
            rhobar = -cosine * alpha
            phi = cosine * phibar
            phibar = sine * phibar
            model = model + phi / rho * w_dir
            w_dir = v_now - theta / rho * w_dir
        v_prev = v_now
        alpha_prev = alpha
    return (model, u_rays)


def solution(mesh):
    return jax.shard_map(
        shards,
        mesh=mesh,
        in_specs=(
            P(("ray", "tile")),
            P("ray", "tile", None, None, None),
            P("ray", "tile", None),
            P("ray", "tile", None),
            P("ray", "tile"),
            P("tile", "ray", None),
        ),
        out_specs=(P("tile", "ray", None), P(("ray", "tile"))),
        check_vma=False,
    )
```

profile of v0, /device:TPU:0, one launch (start us, length us, event | category | flops | bytes accessed | tf_op | source)
XLA Modules:
  0.0 384.9 jit_solution(4923032341245801569)
XLA Ops:
  8.6 14.8 %all_gather.12 = bf16[8192]{0:T(1024)(128)(2,1)S(1)} all-gather(bf16[2048]{0:T(1024)(128)(2,1)S(1)} %get-tuple-element.30), channel_id=1, replica_groups=mesh['ray'=8,'tile'=4] {'tile'}, dimensions={0}, use_global_device_ids=true | all-gather | bytes 20480 | tf_op jit(solution)/shard_map/all_gather | solution.py:74
  25.5 3.4 fusion.6
  28.9 1.7 scatter_custom_fusion
  32.0 3.0 collective-permute-start
  37.1 4.5 %collective-permute-start.3 = (f32[1,10,128]{2,1,0:T(8,128)S(1)}, f32[1,10,128]{2,1,0:T(8,128)S(1)}, u32[]{:S(2)}, u32[]{:S(2)}) collective-permute-start(f32[1,10,128]{2,1,0:T(8,128)S(1)} %get-tuple-element.20), channel_id=1, source_target_pairs={{0,1},{1,2},{2,3},{4,5},{5,6},{6,7},{8,9},{9,10},{10,11},{12,13},{... | collective-permute-start | bytes 15368 | tf_op jit(solution)/shard_map/ppermute | solution.py:20
  41.7 42.2 %psum.35 = f32[]{:T(128)} all-reduce(f32[]{:T(128)} %get-tuple-element.31), channel_id=1, replica_groups=mesh['ray'=8,'tile'=4] {'ray','tile'}, use_global_device_ids=true, to_apply=%region_3.4 | all-reduce | flops 1 | bytes 8 | tf_op jit(solution)/shard_map/psum | solution.py:86
  87.5 40.2 %psum.36 = f32[]{:T(128)} all-reduce(f32[]{:T(128)} %get-tuple-element.12), channel_id=1, replica_groups=mesh['ray'=8,'tile'=4] {'ray','tile'}, use_global_device_ids=true, to_apply=%region_5.6 | all-reduce | flops 1 | bytes 8 | tf_op jit(solution)/shard_map/psum | solution.py:88
  128.4 9.9 %all_gather.13 = bf16[4,64,128]{2,1,0:T(8,128)(2,1)S(1)} all-gather(bf16[4,8,128]{2,1,0:T(8,128)(2,1)S(1)} %get-tuple-element.10), channel_id=1, replica_groups=mesh['ray'=8,'tile'=4] {'ray'}, dimensions={1}, use_global_device_ids=true | all-gather | bytes 73728 | tf_op jit(solution)/shard_map/all_gather | solution.py:62
  139.0 4.4 %fusion.4 = f32[128,1,128]{2,1,0:T(1,128)S(1)} fusion(bf16[1,1,128,128,128]{4,3,2,1,0:T(8,128)(2,1)} %param.7, bf16[128,128,1]{1,0,2:T(8,128)(2,1)S(1)} %bitcast.51), kind=kOutput, calls=%fused_computation.12 | convolution fusion | flops 4194304 | bytes 4292608 | tf_op jit(solution)/shard_map/brc,bc->br/dot_general | solution.py:65
  144.6 17.3 %all-reduce.4 = f32[8192]{0:T(1024)S(1)} all-reduce(f32[8192]{0:T(1024)S(1)} %bitcast.57), channel_id=3, replica_groups=mesh['ray'=8,'tile'=4] {'tile'}, use_global_device_ids=true, to_apply=%region_7.8.clone | all-reduce | flops 8192 | bytes 65536
  163.3 3.0 collective-permute-start.4
  168.4 4.5 %collective-permute-start.7 = (f32[1,10,128]{2,1,0:T(8,128)S(1)}, f32[1,10,128]{2,1,0:T(8,128)S(1)}, u32[]{:S(2)}, u32[]{:S(2)}) collective-permute-start(f32[1,10,128]{2,1,0:T(8,128)S(1)} %get-tuple-element.18), channel_id=1, source_target_pairs={{0,1},{1,2},{2,3},{4,5},{5,6},{6,7},{8,9},{9,10},{10,11},{12,13},{... | collective-permute-start | bytes 15368 | tf_op jit(solution)/shard_map/ppermute | solution.py:20
  172.9 13.1 %all_gather.14 = bf16[8192]{0:T(1024)(128)(2,1)S(1)} all-gather(bf16[2048]{0:T(1024)(128)(2,1)S(1)} %convert_element_type.19), channel_id=1, replica_groups=mesh['ray'=8,'tile'=4] {'tile'}, dimensions={0}, use_global_device_ids=true | all-gather | bytes 20480 | tf_op jit(solution)/shard_map/all_gather | solution.py:74
  188.9 3.0 collective-permute-start.8
  192.0 3.4 fusion.2
  198.4 4.5 %collective-permute-start.11 = (f32[1,10,128]{2,1,0:T(8,128)S(1)}, f32[1,10,128]{2,1,0:T(8,128)S(1)}, u32[]{:S(2)}, u32[]{:S(2)}) collective-permute-start(f32[1,10,128]{2,1,0:T(8,128)S(1)} %get-tuple-element.16), channel_id=1, source_target_pairs={{0,1},{1,2},{2,3},{4,5},{5,6},{6,7},{8,9},{9,10},{10,11},{12,13},{... | collective-permute-start | bytes 15368 | tf_op jit(solution)/shard_map/ppermute | solution.py:20
  204.2 39.7 %psum.37 = f32[]{:T(128)} all-reduce(f32[]{:T(128)S(6)} %add.169), channel_id=1, replica_groups=mesh['ray'=8,'tile'=4] {'ray','tile'}, use_global_device_ids=true, to_apply=%region_10.11 | all-reduce | flops 1 | bytes 8 | tf_op jit(solution)/shard_map/psum | solution.py:86
  246.4 41.6 %psum.38 = f32[]{:T(128)} all-reduce(f32[]{:T(128)} %get-tuple-element.4), channel_id=1, replica_groups=mesh['ray'=8,'tile'=4] {'ray','tile'}, use_global_device_ids=true, to_apply=%region_14.15 | all-reduce | flops 1 | bytes 8 | tf_op jit(solution)/shard_map/psum | solution.py:88
  288.7 9.9 %all_gather.15 = bf16[4,64,128]{2,1,0:T(8,128)(2,1)S(1)} all-gather(bf16[4,8,128]{2,1,0:T(8,128)(2,1)S(1)} %get-tuple-element.2), channel_id=1, replica_groups=mesh['ray'=8,'tile'=4] {'ray'}, dimensions={1}, use_global_device_ids=true | all-gather | bytes 73728 | tf_op jit(solution)/shard_map/all_gather | solution.py:62
  299.3 4.4 %fusion = f32[128,1,128]{2,1,0:T(1,128)S(1)} fusion(bf16[1,1,128,128,128]{4,3,2,1,0:T(8,128)(2,1)} %param.7, bf16[128,128,1]{1,0,2:T(8,128)(2,1)S(1)} %bitcast.49), kind=kOutput, calls=%fused_computation.8 | convolution fusion | flops 4194304 | bytes 4292608 | tf_op jit(solution)/shard_map/brc,bc->br/dot_general | solution.py:65
  306.3 3.0 collective-permute-start.12
  309.4 17.2 %all-reduce.5 = f32[8192]{0:T(1024)S(1)} all-reduce(f32[8192]{0:T(1024)S(1)} %bitcast.56), channel_id=5, replica_groups=mesh['ray'=8,'tile'=4] {'tile'}, use_global_device_ids=true, to_apply=%region_16.17.clone | all-reduce | flops 8192 | bytes 65536
  327.9 4.5 %collective-permute-start.15 = (f32[1,10,128]{2,1,0:T(8,128)S(1)}, f32[1,10,128]{2,1,0:T(8,128)S(1)}, u32[]{:S(2)}, u32[]{:S(2)}) collective-permute-start(f32[1,10,128]{2,1,0:T(8,128)S(1)} %get-tuple-element.14), channel_id=1, source_target_pairs={{0,1},{1,2},{2,3},{4,5},{5,6},{6,7},{8,9},{9,10},{10,11},{12,13},{... | collective-permute-start | bytes 15368 | tf_op jit(solution)/shard_map/ppermute | solution.py:20
  335.9 40.1 %psum.39 = f32[]{:T(128)} all-reduce(f32[]{:T(128)S(6)} %add.184), channel_id=1, replica_groups=mesh['ray'=8,'tile'=4] {'ray','tile'}, use_global_device_ids=true, to_apply=%region_19.20 | all-reduce | flops 1 | bytes 8 | tf_op jit(solution)/shard_map/psum | solution.py:86
  (77 shorter events, 29.0 us)
Async XLA Ops:
  7.2 77.5 %copy-start.3 = (u32[32]{0:T(128)S(1)}, u32[32]{0:T(128)}, u32[]{:S(2)}) copy-start(u32[32]{0:T(128)} %constant.34) | copy-start | bytes 388
  7.2 21.7 %copy-start.2 = (s32[1,1,128]{2,1,0:T(1,128)S(1)}, s32[1,1,128]{2,1,0:T(1,128)}, u32[]{:S(2)}) copy-start(s32[1,1,128]{2,1,0:T(1,128)} %param.8) | copy-start | bytes 1540
  7.2 23.4 %copy-start = (f32[4,8,128]{2,1,0:T(8,128)S(1)}, f32[4,8,128]{2,1,0:T(8,128)}, u32[]{:S(2)}) copy-start(f32[4,8,128]{2,1,0:T(8,128)} %param.11) | copy-start | bytes 49156
  7.2 78.8 %reduce-scatter.3.cloned.1.call-start = ((), (), s32[]{:S(2)}) async-start(), calls=%async_computation.2 | async-start | bytes 147456 | tf_op jit(solution)/shard_map/reduce_scatter | solution.py:83
  25.5 140.8 %copy-start.1 = (f32[2048]{0:T(1024)S(1)}, f32[2048]{0:T(1024)}, u32[]{:S(2)}) copy-start(f32[2048]{0:T(1024)} %param.6) | copy-start | bytes 24580
  30.6 214.4 %reduce-scatter.5.cloned.1.call-start = ((), (), s32[]{:S(2)}) async-start(), calls=%async_computation.3 | async-start | bytes 147456 | tf_op jit(solution)/shard_map/reduce_scatter | solution.py:83
  30.7 4.4 %collective-permute-start.1 = (f32[4,1,128]{2,1,0:T(1,128)S(1)}, f32[4,1,128]{2,1,0:T(1,128)S(1)}, u32[]{:S(2)}, u32[]{:S(2)}) collective-permute-start(f32[4,1,128]{2,1,0:T(1,128)S(1)} %get-tuple-element.29), channel_id=1, source_target_pairs={{4,0},{8,4},{12,8},{16,12},{20,16},{24,20},{28,24},{5,1},{9,5},{13... | collective-permute-start | bytes 6152 | tf_op jit(solution)/shard_map/ppermute | solution.py:22
  32.0 3.8 collective-permute-start
  35.8 50.1 %collective-permute-start.2 = (f32[1,10,128]{2,1,0:T(8,128)S(1)}, f32[1,10,128]{2,1,0:T(8,128)S(1)}, u32[]{:S(2)}, u32[]{:S(2)}) collective-permute-start(f32[1,10,128]{2,1,0:T(8,128)S(1)} %get-tuple-element.21), channel_id=1, source_target_pairs={{1,0},{2,1},{3,2},{5,4},{6,5},{7,6},{9,8},{10,9},{11,10},{13,12},{... | collective-permute-start | bytes 15368 | tf_op jit(solution)/shard_map/ppermute | solution.py:22
  37.1 48.8 %collective-permute-start.3 = (f32[1,10,128]{2,1,0:T(8,128)S(1)}, f32[1,10,128]{2,1,0:T(8,128)S(1)}, u32[]{:S(2)}, u32[]{:S(2)}) collective-permute-start(f32[1,10,128]{2,1,0:T(8,128)S(1)} %get-tuple-element.20), channel_id=1, source_target_pairs={{0,1},{1,2},{2,3},{4,5},{5,6},{6,7},{8,9},{9,10},{10,11},{12,13},{... | collective-permute-start | bytes 15368 | tf_op jit(solution)/shard_map/ppermute | solution.py:20
  162.0 5.0 %collective-permute-start.5 = (f32[4,1,128]{2,1,0:T(1,128)S(1)}, f32[4,1,128]{2,1,0:T(1,128)S(1)}, u32[]{:S(2)}, u32[]{:S(2)}) collective-permute-start(f32[4,1,128]{2,1,0:T(1,128)S(1)} %get-tuple-element.27), channel_id=1, source_target_pairs={{4,0},{8,4},{12,8},{16,12},{20,16},{24,20},{28,24},{5,1},{9,5},{13... | collective-permute-start | bytes 6152 | tf_op jit(solution)/shard_map/ppermute | solution.py:22
  163.3 3.8 collective-permute-start.4
  167.1 19.7 %collective-permute-start.6 = (f32[1,10,128]{2,1,0:T(8,128)S(1)}, f32[1,10,128]{2,1,0:T(8,128)S(1)}, u32[]{:S(2)}, u32[]{:S(2)}) collective-permute-start(f32[1,10,128]{2,1,0:T(8,128)S(1)} %get-tuple-element.19), channel_id=1, source_target_pairs={{1,0},{2,1},{3,2},{5,4},{6,5},{7,6},{9,8},{10,9},{11,10},{13,12},{... | collective-permute-start | bytes 15368 | tf_op jit(solution)/shard_map/ppermute | solution.py:22
  168.4 18.4 %collective-permute-start.7 = (f32[1,10,128]{2,1,0:T(8,128)S(1)}, f32[1,10,128]{2,1,0:T(8,128)S(1)}, u32[]{:S(2)}, u32[]{:S(2)}) collective-permute-start(f32[1,10,128]{2,1,0:T(8,128)S(1)} %get-tuple-element.18), channel_id=1, source_target_pairs={{0,1},{1,2},{2,3},{4,5},{5,6},{6,7},{8,9},{9,10},{10,11},{12,13},{... | collective-permute-start | bytes 15368 | tf_op jit(solution)/shard_map/ppermute | solution.py:20
  187.6 9.4 %collective-permute-start.9 = (f32[4,1,128]{2,1,0:T(1,128)S(1)}, f32[4,1,128]{2,1,0:T(1,128)S(1)}, u32[]{:S(2)}, u32[]{:S(2)}) collective-permute-start(f32[4,1,128]{2,1,0:T(1,128)S(1)} %get-tuple-element.25), channel_id=1, source_target_pairs={{4,0},{8,4},{12,8},{16,12},{20,16},{24,20},{28,24},{5,1},{9,5},{13... | collective-permute-start | bytes 6152 | tf_op jit(solution)/shard_map/ppermute | solution.py:22
  188.9 8.1 %collective-permute-start.8 = (f32[4,1,128]{2,1,0:T(1,128)S(1)}, f32[4,1,128]{2,1,0:T(1,128)S(1)}, u32[]{:S(2)}, u32[]{:S(2)}) collective-permute-start(f32[4,1,128]{2,1,0:T(1,128)S(1)} %get-tuple-element.24), channel_id=1, source_target_pairs={{0,4},{4,8},{8,12},{12,16},{16,20},{20,24},{24,28},{1,5},{5,9},{9,... | collective-permute-start | bytes 6152 | tf_op jit(solution)/shard_map/ppermute | solution.py:20
  197.1 47.7 %collective-permute-start.10 = (f32[1,10,128]{2,1,0:T(8,128)S(1)}, f32[1,10,128]{2,1,0:T(8,128)S(1)}, u32[]{:S(2)}, u32[]{:S(2)}) collective-permute-start(f32[1,10,128]{2,1,0:T(8,128)S(1)} %get-tuple-element.17), channel_id=1, source_target_pairs={{1,0},{2,1},{3,2},{5,4},{6,5},{7,6},{9,8},{10,9},{11,10},{13,12},{... | collective-permute-start | bytes 15368 | tf_op jit(solution)/shard_map/ppermute | solution.py:22
  198.4 46.4 %collective-permute-start.11 = (f32[1,10,128]{2,1,0:T(8,128)S(1)}, f32[1,10,128]{2,1,0:T(8,128)S(1)}, u32[]{:S(2)}, u32[]{:S(2)}) collective-permute-start(f32[1,10,128]{2,1,0:T(8,128)S(1)} %get-tuple-element.16), channel_id=1, source_target_pairs={{0,1},{1,2},{2,3},{4,5},{5,6},{6,7},{8,9},{9,10},{10,11},{12,13},{... | collective-permute-start | bytes 15368 | tf_op jit(solution)/shard_map/ppermute | solution.py:20
  305.0 21.5 %collective-permute-start.13 = (f32[4,1,128]{2,1,0:T(1,128)S(1)}, f32[4,1,128]{2,1,0:T(1,128)S(1)}, u32[]{:S(2)}, u32[]{:S(2)}) collective-permute-start(f32[4,1,128]{2,1,0:T(1,128)S(1)} %get-tuple-element.23), channel_id=1, source_target_pairs={{4,0},{8,4},{12,8},{16,12},{20,16},{24,20},{28,24},{5,1},{9,5},{13... | collective-permute-start | bytes 6152 | tf_op jit(solution)/shard_map/ppermute | solution.py:22
  306.3 20.2 %collective-permute-start.12 = (f32[4,1,128]{2,1,0:T(1,128)S(1)}, f32[4,1,128]{2,1,0:T(1,128)S(1)}, u32[]{:S(2)}, u32[]{:S(2)}) collective-permute-start(f32[4,1,128]{2,1,0:T(1,128)S(1)} %get-tuple-element.22), channel_id=1, source_target_pairs={{0,4},{4,8},{8,12},{12,16},{16,20},{20,24},{24,28},{1,5},{5,9},{9,... | collective-permute-start | bytes 6152 | tf_op jit(solution)/shard_map/ppermute | solution.py:20
  326.6 6.5 %collective-permute-start.14 = (f32[1,10,128]{2,1,0:T(8,128)S(1)}, f32[1,10,128]{2,1,0:T(8,128)S(1)}, u32[]{:S(2)}, u32[]{:S(2)}) collective-permute-start(f32[1,10,128]{2,1,0:T(8,128)S(1)} %get-tuple-element.15), channel_id=1, source_target_pairs={{1,0},{2,1},{3,2},{5,4},{6,5},{7,6},{9,8},{10,9},{11,10},{13,12},{... | collective-permute-start | bytes 15368 | tf_op jit(solution)/shard_map/ppermute | solution.py:22
  327.9 5.9 %collective-permute-start.15 = (f32[1,10,128]{2,1,0:T(8,128)S(1)}, f32[1,10,128]{2,1,0:T(8,128)S(1)}, u32[]{:S(2)}, u32[]{:S(2)}) collective-permute-start(f32[1,10,128]{2,1,0:T(8,128)S(1)} %get-tuple-element.14), channel_id=1, source_target_pairs={{0,1},{1,2},{2,3},{4,5},{5,6},{6,7},{8,9},{9,10},{10,11},{12,13},{... | collective-permute-start | bytes 15368 | tf_op jit(solution)/shard_map/ppermute | solution.py:20
Sparse Core Ops, SparseCore 0:
  30.7 34.3 reduce-scatter.2
  197.2 33.0 reduce-scatter.4
where the time goes:
time: 387 us; the launch traced here: 385 us
  blocking collectives  286 us (74%)
  starting transfers between devices  40.7 us (11%)
  between operations  22.3 us (6%)
  matrix products  15.6 us (4%)
  other arithmetic  15.1 us (4%)
    psum x3, blocking collectives, shards(): beta = jnp.sqrt(lax.psum(squares, ('ray', 'tile')) + eps)  122 us
    psum x2, blocking collectives, shards(): alpha = jnp.sqrt(lax.psum(jnp.sum(v_raw * v_raw), ('ray', 'tile')) + eps)  81.8 us
    unnamed x2, blocking collectives  34.4 us
    ppermute x8, starting transfers between devices, padded_2(): lax.ppermute(tail, axis, [(i, (i + 1) % count) for i in range(ends)])  30.3 us
    all_gather x2, blocking collectives, shards(): lax.all_gather(raw_rays.astype(jnp.bfloat16), 'tile', axis=0, tiled=True)  27.9 us
    all_gather x2, blocking collectives, shards(): lax.all_gather(v_prev.astype(jnp.bfloat16), 'ray', axis=1, tiled=True)  19.7 us
    ppermute x8, starting transfers between devices, padded_2(): lax.ppermute(head, axis, [((i + 1) % count, i) for i in range(ends)])  10.3 us
    dot_general x2, matrix products, shards(): jnp.einsum('brc,bc->br', values, whole[cols], preferred_element_type=jnp....  8.86 us
  transfers between devices with their start and end apart: 18, of which 3 were waited for; matrix products, arithmetic and copies ran while one was open for 2% of the time, Pallas kernels for 0%

commit v1 on v0

v1 whole, which is shorter than its diff:
```python
import functools

import jax
import jax.numpy as jnp
from jax import lax
from jax.experimental import pallas as pl
from jax.experimental.pallas import tpu as pltpu
from jax.sharding import PartitionSpec as P

MESH = pl.DeviceIdType.MESH
EPS = 1e-06
GROUP = 16
F32 = jnp.float32
BF16 = jnp.bfloat16


def total(x):
    return jnp.sum(jnp.sum(x, axis=0, keepdims=True), axis=1, keepdims=True)


def fold(x):
    acc = x[0:8] * x[0:8]
    for i in range(8, x.shape[0], 8):
        acc = acc + x[i : i + 8] * x[i : i + 8]
    return acc


def dot(a, b):
    return jnp.dot(a, b, preferred_element_type=F32)


def exact_dot(onehot, x):
    p1 = x.astype(BF16)
    rest = x - p1.astype(F32)
    p2 = rest.astype(BF16)
    p3 = (rest - p2.astype(F32)).astype(BF16)
    return dot(onehot, p1) + dot(onehot, p2) + dot(onehot, p3)


def laplace(cur, prev, nxt, xlo, xhi, size_y):
    rows, lanes = cur.shape
    iy = lax.broadcasted_iota(jnp.int32, cur.shape, 0) & (size_y - 1)
    iz = lax.broadcasted_iota(jnp.int32, cur.shape, 1)
    up = jnp.where(iy == 0, pltpu.roll(prev, rows - size_y + 1, 0), pltpu.roll(cur, 1, 0))
    down = jnp.where(
        iy == size_y - 1, pltpu.roll(nxt, size_y - 1, 0), pltpu.roll(cur, rows - 1, 0)
    )
    left = jnp.where(iz == 0, 0.0, pltpu.roll(cur, 1, 1))
    right = jnp.where(iz == lanes - 1, 0.0, pltpu.roll(cur, lanes - 1, 1))
    below = jnp.concatenate([xlo, cur[:-size_y]], axis=0)
    above = jnp.concatenate([cur[size_y:], xhi], axis=0)
    return 6.0 * cur - (above + below + down + up + right + left)


def kernel(
    n_ray,
    n_tile,
    size_x,
    size_y,
    data_ref,
    blocks_ref,
    cols_ref,
    rows_ref,
    count_ref,
    reg_ref,
    model_ref,
    out_ref,
    held,
    pick,
    prod,
    dfull,
    zbuf,
    zrecv,
    vfull,
    vhalo,
    yrecv,
    small,
    qbuf,
    qhalo_y,
    qhalo_x,
    last,
    ubuf,
    block_sem,
    a_send,
    a_recv,
    b_send,
    b_recv,
    d_send,
    d_recv,
    h_send,
    h_recv,
    e_send,
    e_recv,
    s_send,
    s_recv,
    q_send,
    q_recv,
    f_send,
    f_recv,
):
    me = lax.axis_index("ray")
    t = lax.axis_index("tile")
    slots, width, depth = held.shape
    cells = size_x * size_y
    tile_cols = n_ray * cells
    grid_y = n_ray * size_y
    share = data_ref.shape[0]
    row_blocks = share * n_tile
    groups = slots // GROUP

    def block_copy(g):
        part = pl.ds(g * GROUP, GROUP)
        return pltpu.make_async_copy(blocks_ref.at[part], held.at[part], block_sem.at[g])

    for g in range(groups):
        block_copy(g).start()

    def ray_peer(d):
        return lax.rem(me + d, n_ray)

    def tile_peer(d):
        return lax.rem(t + d, n_tile)

    bar = pltpu.get_barrier_semaphore()
    for d in range(1, n_ray):
        pl.semaphore_signal(bar, inc=1, device_id=(ray_peer(d), t), device_id_type=MESH)
    for d in range(1, n_tile):
        pl.semaphore_signal(bar, inc=1, device_id=(me, tile_peer(d)), device_id_type=MESH)
    pl.semaphore_wait(bar, n_ray + n_tile - 2)

    started = []

    def send(src, dst, send_sem, recv_sem, device):
        copy = pltpu.make_async_remote_copy(
            src_ref=src,
            dst_ref=dst,
            send_sem=send_sem,
            recv_sem=recv_sem,
            device_id=device,
            device_id_type=MESH,
        )
        copy.start()
        started.append(copy)
        return copy

    def to_tiles(ref, sends, recvs):
        return [
            send(ref, ref, sends.at[d - 1], recvs.at[d - 1], (me, tile_peer(d)))
            for d in range(1, n_tile)
        ]

    def to_rays(ref, sends, recvs):
        return [
            send(ref, ref, sends.at[d - 1], recvs.at[d - 1], (ray_peer(d), t))
            for d in range(1, n_ray)
        ]

    def arrived(copies):
        for copy in copies:
            copy.wait_recv()

    mine = pl.ds(pl.multiple_of(t * share, share), share)
    dfull[mine, :] = data_ref[...]
    copies = to_tiles(dfull.at[mine], a_send, a_recv)

    live = lax.broadcasted_iota(jnp.int32, (1, slots), 1) < count_ref[...]
    col = cols_ref[...]
    col_x = lax.shift_right_logical(col, grid_y.bit_length() - 1)
    col_y = col & (grid_y - 1)
    place = (
        lax.shift_right_logical(col_y, size_y.bit_length() - 1) * cells
        + col_x * size_y
        + (col_y & (size_y - 1))
    )
    place = jnp.where(live, place, -1)
    row = jnp.where(live, rows_ref[...], -1)
    to_col = jnp.where(
        lax.broadcasted_iota(jnp.int32, (tile_cols, slots), 0) == place, 1.0, 0.0
    ).astype(F32)
    to_row = jnp.where(
        lax.broadcasted_iota(jnp.int32, (row_blocks, slots), 0) == row, 1.0, 0.0
    ).astype(F32)
    from_col = to_col.T.astype(BF16)
    from_row = to_row.T.astype(BF16)
    to_col = to_col.astype(BF16)
    to_row = to_row.astype(BF16)
    reg = reg_ref[...]
    has_prev = jnp.where(me > 0, 1.0, 0.0).astype(F32)
    has_next = jnp.where(me < n_ray - 1, 1.0, 0.0).astype(F32)
    has_below = jnp.where(t > 0, 1.0, 0.0).astype(F32)
    has_above = jnp.where(t < n_tile - 1, 1.0, 0.0).astype(F32)

    def transposed(half, first):
        pick[0] = dot(from_row, half).astype(BF16)
        sub = lax.broadcasted_iota(jnp.int32, (GROUP, depth), 0)

        @pl.loop(0, groups)
        def _(g):
            if first:
                block_copy(g).wait()
            start = pl.multiple_of(g * GROUP, GROUP)
            lhs = pick[0, pl.ds(start, GROUP), :]
            acc = jnp.zeros((GROUP, depth), F32)
            for j in range(GROUP):
                acc = jnp.where(sub == j, dot(lhs, held[start + j]), acc)
            prod[pl.ds(start, GROUP), :] = acc

        return exact_dot(to_col, prod[...])

    def forward(field):
        hi = field.astype(BF16)
        lo = (field - hi.astype(F32)).astype(BF16)
        pick[0] = dot(from_col, hi).astype(BF16)
        pick[1] = dot(from_col, lo).astype(BF16)
        sub = lax.broadcasted_iota(jnp.int32, (2 * GROUP, width), 0) & (GROUP - 1)

        @pl.loop(0, groups)
        def _(g):
            start = pl.multiple_of(g * GROUP, GROUP)
            lhs = jnp.concatenate(
                [pick[0, pl.ds(start, GROUP), :], pick[1, pl.ds(start, GROUP), :]], axis=0
            )
            acc = jnp.zeros((2 * GROUP, width), F32)
            for j in range(GROUP):
                one = lax.dot_general(
                    lhs, held[start + j], (((1,), (1,)), ((), ())), preferred_element_type=F32
                )
                acc = jnp.where(sub == j, one, acc)
            prod[pl.ds(start, GROUP), :] = acc[:GROUP] + acc[GROUP:]

        return exact_dot(to_row, prod[...])

    def spread_z(s, z, squares):
        for p in range(n_ray):
            zbuf[s, p, 0:cells, :] = z[p * cells : (p + 1) * cells]
            zbuf[s, p, cells : cells + 8, :] = squares
        zrecv[s, me] = zbuf[s, me]
        return [
            send(
                zbuf.at[s, ray_peer(d)],
                zrecv.at[s, me],
                b_send.at[s, d - 1],
                b_recv.at[s, d - 1],
                (ray_peer(d), t),
            )
            for d in range(1, n_ray)
        ]

    def summed(ref, count):
        acc = ref[0]
        for i in range(1, count):
            acc = acc + ref[i]
        return acc

    own = pl.ds(pl.multiple_of(me * cells, cells), cells)
    before = pl.ds(pl.multiple_of(ray_peer(n_ray - 1) * cells, cells), cells)
    after = pl.ds(pl.multiple_of(ray_peer(1) * cells, cells), cells)

    def edges(ref, dst, sends, recvs):
        return [
            send(
                ref.at[pl.ds(cells - size_y, size_y)],
                dst.at[0],
                sends.at[0],
                recvs.at[0],
                (me, tile_peer(1)),
            ),
            send(
                ref.at[pl.ds(0, size_y)],
                dst.at[1],
                sends.at[1],
                recvs.at[1],
                (me, tile_peer(n_tile - 1)),
            ),
        ]

    arrived(copies)
    raw_rays = dfull[...]
    old_rays = None
    raw_cells = None
    v_prev = None
    for s in range(3):
        if s < 2:
            z = transposed(raw_rays.astype(BF16), s == 0)
            squares = fold(raw_rays)
            if s > 0:
                arrived(cell_copies)
                squares = squares + summed(small.at[1], n_tile)
            copies = spread_z(s, z, squares)
            if s > 0:
                arrived(q_copies)
                smooth = laplace(
                    qbuf[...],
                    qhalo_y[0] * has_prev,
                    qhalo_y[1] * has_next,
                    qhalo_x[0] * has_below,
                    qhalo_x[1] * has_above,
                    size_y,
                )
            arrived(copies)
            sums = summed(zrecv.at[s], n_ray)
            beta = jnp.sqrt(total(sums[cells:]) + EPS)
            if s == 0:
                v_raw = sums[:cells] / beta
            else:
                v_raw = (sums[:cells] + smooth) / beta - beta * v_prev
            field = vfull.at[s]
            field[own, :] = v_raw
            copies = to_rays(field.at[own], d_send.at[s], d_recv.at[s])
            halo_copies = edges(
                field.at[own], vhalo.at[s], h_send.at[s], h_recv.at[s]
            )
            arrived(copies)
            whole = field[...]
            small[2 * s, t] = fold(whole)
            alpha_copies = to_tiles(small.at[2 * s, t], s_send.at[2 * s], s_recv.at[2 * s])
            yrecv[s, t] = forward(whole)
            y_copies = to_tiles(yrecv.at[s, t], e_send.at[s], e_recv.at[s])
            arrived(halo_copies)
            smooth_v = reg * laplace(
                v_raw,
                field[before, :] * has_prev,
                field[after, :] * has_next,
                vhalo[s, 0] * has_below,
                vhalo[s, 1] * has_above,
                size_y,
            )
            arrived(alpha_copies)
            alpha = jnp.sqrt(total(summed(small.at[2 * s], n_tile)) + EPS)
            v_now = v_raw / alpha
            if s == 0:
                new_cells = smooth_v / alpha
            else:
                new_cells = smooth_v / alpha - alpha * (raw_cells / beta)
            small[2 * s + 1, t] = fold(new_cells)
            cell_copies = to_tiles(
                small.at[2 * s + 1, t], s_send.at[2 * s + 1], s_recv.at[2 * s + 1]
            )
            if s == 0:
                qbuf[...] = reg * new_cells
                q_copies = edges(qbuf, qhalo_x, q_send, q_recv) + [
                    send(
                        qbuf, qhalo_y.at[0], q_send.at[2], q_recv.at[2], (ray_peer(1), t)
                    ),
                    send(
                        qbuf,
                        qhalo_y.at[1],
                        q_send.at[3],
                        q_recv.at[3],
                        (ray_peer(n_ray - 1), t),
                    ),
                ]
            old_rays = raw_rays / beta
            if s == 0:
                w_dir = v_now
                phibar = beta
                rhobar = alpha
                model = None
            else:
                rho = jnp.sqrt(rhobar * rhobar + beta * beta)
                cosine = rhobar / rho
                sine = beta / rho
                theta = sine * alpha
                rhobar = -cosine * alpha
                phi = cosine * phibar
                phibar = sine * phibar
                model = phi / rho * w_dir
                w_dir = v_now - theta / rho * w_dir
            arrived(y_copies)
            raw_rays = summed(yrecv.at[s], n_tile) / alpha - alpha * old_rays
            raw_cells = new_cells
            v_prev = v_now
        else:
            arrived(cell_copies)
            last[me] = fold(raw_rays) + summed(small.at[3], n_tile)
            copies = to_rays(last.at[me], f_send, f_recv)
            arrived(copies)
            beta = jnp.sqrt(total(summed(last, n_ray)) + EPS)
            ubuf[...] = raw_rays
            out_ref[...] = ubuf[mine, :] / beta
            rho = jnp.sqrt(rhobar * rhobar + beta * beta)
            phi = rhobar / rho * phibar
            model_ref[...] = model + phi / rho * w_dir
    for copy in started:
        copy.wait_send()


def shards(n_ray, n_tile, data, blocks, block_cols, block_rows, block_counts, reg_weight):
    size_x, size_y, depth = reg_weight.shape
    slots, width = blocks.shape[2:4]
    cells = size_x * size_y
    share = data.shape[0] // width
    row_blocks = share * n_tile
    dma = pltpu.SemaphoreType.DMA
    pairs = [
        dma((n_tile - 1,)),
        dma((n_tile - 1,)),
        dma((2, n_ray - 1)),
        dma((2, n_ray - 1)),
        dma((2, n_ray - 1)),
        dma((2, n_ray - 1)),
        dma((2, 2)),
        dma((2, 2)),
        dma((2, n_tile - 1)),
        dma((2, n_tile - 1)),
        dma((4, n_tile - 1)),
        dma((4, n_tile - 1)),
        dma((4,)),
        dma((4,)),
        dma((n_ray - 1,)),
        dma((n_ray - 1,)),
    ]
    vmem = pl.BlockSpec(memory_space=pltpu.VMEM)
    model, rays = pl.pallas_call(
        functools.partial(kernel, n_ray, n_tile, size_x, size_y),
        out_shape=(
            jax.ShapeDtypeStruct((cells, depth), F32),
            jax.ShapeDtypeStruct((share, width), F32),
        ),
        in_specs=[vmem, pl.BlockSpec(memory_space=pl.ANY), vmem, vmem, vmem, vmem],
        out_specs=(vmem, vmem),
        scratch_shapes=[
            pltpu.VMEM((slots, width, depth), BF16),
            pltpu.VMEM((2, slots, depth), BF16),
            pltpu.VMEM((slots, depth), F32),
            pltpu.VMEM((row_blocks, width), F32),
            pltpu.VMEM((2, n_ray, cells + 8, depth), F32),
            pltpu.VMEM((2, n_ray, cells + 8, depth), F32),
            pltpu.VMEM((2, n_ray * cells, depth), F32),
            pltpu.VMEM((2, 2, size_y, depth), F32),
            pltpu.VMEM((2, n_tile, row_blocks, width), F32),
            pltpu.VMEM((4, n_tile, 8, depth), F32),
            pltpu.VMEM((cells, depth), F32),
            pltpu.VMEM((2, cells, depth), F32),
            pltpu.VMEM((2, size_y, depth), F32),
            pltpu.VMEM((n_ray, 8, depth), F32),
            pltpu.VMEM((row_blocks, width), F32),
            dma((slots // GROUP,)),
        ]
        + pairs,
        compiler_params=pltpu.CompilerParams(
            collective_id=0, has_side_effects=True, vmem_limit_bytes=48 * 2**20
        ),
    )(
        data.reshape(share, width),
        blocks.reshape(slots, width, depth),
        block_cols.reshape(1, slots),
        block_rows.reshape(1, slots),
        block_counts,
        reg_weight.reshape(cells, depth),
    )
    return model.reshape(size_x, size_y, depth), rays.reshape(-1)


def solution(mesh):
    return jax.shard_map(
        functools.partial(shards, mesh.shape["ray"], mesh.shape["tile"]),
        mesh=mesh,
        in_specs=(
            P(("ray", "tile")),
            P("ray", "tile", None, None, None),
            P("ray", "tile", None),
            P("ray", "tile", None),
            P("ray", "tile"),
            P("tile", "ray", None),
        ),
        out_specs=(P("tile", "ray", None), P(("ray", "tile"))),
        check_vma=False,
    )
```

time: 387 us -> 57.9 us (0.15)
  blocking collectives: 286 us -> 0 us
  Pallas kernels: 0 us -> 50.2 us
  starting transfers between devices: 40.7 us -> 0 us
  between operations: 22.3 us -> 1.3 us
  matrix products: 15.6 us -> 0 us
  other arithmetic: 15.1 us -> 0 us
    psum x5 -> x0, blocking collectives: 204 us -> none  [the longest x3 122 us: shards(): beta = jnp.sqrt(lax.psum(squares, ('ray', 'tile')) + eps)]
    pallas_call x0 -> x1, Pallas kernels: none -> 50.2 us  [shards(): pl.pallas_call(functools.partial(kernel, n_ray, n_tile, size_x, size_y),...]
    all_gather x4 -> x0, blocking collectives: 47.7 us -> none  [the longest x2 27.9 us: shards(): lax.all_gather(raw_rays.astype(jnp.bfloat16), 'tile', axis=0, tiled=True)]
    ppermute x16 -> x0, starting transfers between devices: 40.6 us -> none  [the longest x8 30.3 us: padded_2(): lax.ppermute(tail, axis, [(i, (i + 1) % count) for i in range(ends)])]
    unnamed x2 -> x0, blocking collectives: 34.4 us -> none
    dot_general x4 -> x0, matrix products: 15.6 us -> none  [the longest x2 8.86 us: shards(): jnp.einsum('brc,bc->br', values, whole[cols], preferred_element_type=jnp....]
    scatter-add x4 -> x0, other arithmetic: 5.88 us -> none  [the longest x2 3.37 us: shards(): jax.ops.segment_sum(jnp.where(live, contrib, 0.0), cols, num_segments=til...]
    unnamed x9 -> x12, local copies, waits for them, and re-layouts: 0.6 us -> 6.11 us
  transfers between devices with their start and end apart: 18 -> 0, of which waited for: 3 -> 0; matrix products, arithmetic and copies ran while one was open for 2% -> 0% of each run, Pallas kernels for 0% -> 0%
where the time goes in v1:
time: 57.9 us; the launch traced here: 57.6 us
  Pallas kernels  50.2 us (87%)
  local copies, waits for them, and re-layouts  6.11 us (11%)
  between operations  1.3 us (2%)
    pallas_call x1, Pallas kernels, shards(): pl.pallas_call(functools.partial(kernel, n_ray, n_tile, size_x, size_y),...  50.2 us
    unnamed x12, local copies, waits for them, and re-layouts  6.11 us

profile of v1, /device:TPU:0, one launch (start us, length us, event | category | flops | bytes accessed | tf_op | source)
XLA Modules:
  0.0 57.6 jit_solution(13796951005438727677)
XLA Ops:
  1.3 0.0 copy-start
  1.3 2.2 %copy-done = bf16[1,1,128,128,128]{4,3,2,1,0:T(8,128)(2,1)S(1)} copy-done((bf16[1,1,128,128,128]{4,3,2,1,0:T(8,128)(2,1)S(1)}, bf16[1,1,128,128,128]{4,3,2,1,0:T(8,128)(2,1)}, u32[]{:S(2)}) %copy-start) | copy-done | bytes 4194328
  3.5 0.0 copy-start.1
  3.5 0.7 %copy-done.1 = f32[4,8,128]{2,1,0:T(8,128)S(1)} copy-done((f32[4,8,128]{2,1,0:T(8,128)S(1)}, f32[4,8,128]{2,1,0:T(8,128)}, u32[]{:S(2)}) %copy-start.1) | copy-done | bytes 16408
  4.2 0.0 copy-start.2
  4.2 0.7 %copy-done.2 = f32[2048]{0:T(1024)S(1)} copy-done((f32[2048]{0:T(1024)S(1)}, f32[2048]{0:T(1024)}, u32[]{:S(2)}) %copy-start.2) | copy-done | bytes 8216
  4.9 0.0 copy-start.3
  4.9 0.7 %copy-done.3 = s32[1,1,128]{2,1,0:T(1,128)S(1)} copy-done((s32[1,1,128]{2,1,0:T(1,128)S(1)}, s32[1,1,128]{2,1,0:T(1,128)}, u32[]{:S(2)}) %copy-start.3) | copy-done | bytes 536
  5.5 0.0 copy-start.4
  5.5 0.7 %copy-done.4 = s32[1,1,128]{2,1,0:T(1,128)S(1)} copy-done((s32[1,1,128]{2,1,0:T(1,128)S(1)}, s32[1,1,128]{2,1,0:T(1,128)}, u32[]{:S(2)}) %copy-start.4) | copy-done | bytes 536
  6.2 50.2 %shard_map.77 = (f32[32,128]{1,0:T(8,128)S(1)}, f32[16,128]{1,0:T(8,128)S(1)}) custom-call(f32[16,128]{1,0:T(8,128)S(1)} %bitcast.10, bf16[128,128,128]{2,1,0:T(8,128)(2,1)S(1)} %bitcast.7, s32[1,128]{1,0:T(1,128)S(1)} %bitcast.12, s32[1,128]{1,0:T(1,128)S(1)} %bitcast.13, s32[1,1]{1,0:T(1,128)S(6)} %copy.10.count_ref, f32[32,128]{1,0:T(8,128)S(1)} %bitcast.8), custom_call_target="tpu_custom_call" | custom-call | tf_op jit(solution)/shard_map/pallas_call | solution.py:414
  56.4 0.6 %copy.11 = f32[4,8,128]{2,1,0:T(8,128)} copy(f32[4,8,128]{2,1,0:T(8,128)S(1)} %bitcast.9) | data formatting | bytes 32768
  57.0 0.6 %copy.12 = f32[2048]{0:T(1024)} copy(f32[2048]{0:T(1024)S(1)} %bitcast.11) | data formatting | bytes 16384
Async XLA Ops:
  1.3 2.2 %copy-start = (bf16[1,1,128,128,128]{4,3,2,1,0:T(8,128)(2,1)S(1)}, bf16[1,1,128,128,128]{4,3,2,1,0:T(8,128)(2,1)}, u32[]{:S(2)}) copy-start(bf16[1,1,128,128,128]{4,3,2,1,0:T(8,128)(2,1)} %param.7) | copy-start | bytes 12582916
  3.5 0.7 %copy-start.1 = (f32[4,8,128]{2,1,0:T(8,128)S(1)}, f32[4,8,128]{2,1,0:T(8,128)}, u32[]{:S(2)}) copy-start(f32[4,8,128]{2,1,0:T(8,128)} %param.11) | copy-start | bytes 49156
  4.2 0.7 %copy-start.2 = (f32[2048]{0:T(1024)S(1)}, f32[2048]{0:T(1024)}, u32[]{:S(2)}) copy-start(f32[2048]{0:T(1024)} %param.6) | copy-start | bytes 24580
  4.9 0.7 %copy-start.3 = (s32[1,1,128]{2,1,0:T(1,128)S(1)}, s32[1,1,128]{2,1,0:T(1,128)}, u32[]{:S(2)}) copy-start(s32[1,1,128]{2,1,0:T(1,128)} %param.8) | copy-start | bytes 1540
  5.5 0.7 %copy-start.4 = (s32[1,1,128]{2,1,0:T(1,128)S(1)}, s32[1,1,128]{2,1,0:T(1,128)}, u32[]{:S(2)}) copy-start(s32[1,1,128]{2,1,0:T(1,128)} %param.9) | copy-start | bytes 1540

commit v2 on v1

--- a/solution.py
+++ b/solution.py
@@ -57,14 +57,18 @@
     n_tile,
     size_x,
     size_y,
-    data_ref,
+    data_hbm,
     blocks_ref,
+    cols_hbm,
+    rows_hbm,
+    count_hbm,
+    reg_hbm,
+    model_ref,
+    out_ref,
     cols_ref,
     rows_ref,
     count_ref,
     reg_ref,
-    model_ref,
-    out_ref,
     held,
     pick,
     prod,
@@ -80,6 +84,7 @@
     qhalo_x,
     last,
     ubuf,
+    in_sem,
     block_sem,
     a_send,
     a_recv,
@@ -104,7 +109,7 @@
     cells = size_x * size_y
     tile_cols = n_ray * cells
     grid_y = n_ray * size_y
-    share = data_ref.shape[0]
+    share = data_hbm.shape[0]
     row_blocks = share * n_tile
     groups = slots // GROUP
 
@@ -112,6 +117,21 @@
         part = pl.ds(g * GROUP, GROUP)
         return pltpu.make_async_copy(blocks_ref.at[part], held.at[part], block_sem.at[g])
 
+    mine = pl.ds(pl.multiple_of(t * share, share), share)
+    inputs = [
+        pltpu.make_async_copy(src, dst, in_sem.at[i])
+        for i, (src, dst) in enumerate(
+            [
+                (data_hbm, dfull.at[mine]),
+                (cols_hbm, cols_ref),
+                (rows_hbm, rows_ref),
+                (count_hbm, count_ref),
+                (reg_hbm, reg_ref),
+            ]
+        )
+    ]
+    for copy in inputs:
+        copy.start()
     for g in range(groups):
         block_copy(g).start()
 
@@ -159,10 +179,11 @@
         for copy in copies:
             copy.wait_recv()
 
-    mine = pl.ds(pl.multiple_of(t * share, share), share)
-    dfull[mine, :] = data_ref[...]
+    inputs[0].wait()
     copies = to_tiles(dfull.at[mine], a_send, a_recv)
 
+    for copy in inputs[1:]:
+        copy.wait()
     live = lax.broadcasted_iota(jnp.int32, (1, slots), 1) < count_ref[...]
     col = cols_ref[...]
     col_x = lax.shift_right_logical(col, grid_y.bit_length() - 1)
@@ -191,18 +212,33 @@
     has_above = jnp.where(t < n_tile - 1, 1.0, 0.0).astype(F32)
 
     def transposed(half, first):
-        pick[0] = dot(from_row, half).astype(BF16)
+        pick[...] = dot(from_row, half).astype(BF16)
         sub = lax.broadcasted_iota(jnp.int32, (GROUP, depth), 0)
+        upper = (sub & 3) < 2
+        even = (sub & 1) == 0
+        quad = lax.shift_right_logical(sub, 2)
 
         @pl.loop(0, groups)
         def _(g):
             if first:
                 block_copy(g).wait()
             start = pl.multiple_of(g * GROUP, GROUP)
-            lhs = pick[0, pl.ds(start, GROUP), :]
+            lhs = pick[pl.ds(start, GROUP), :].astype(F32)
+            lhs = jnp.concatenate(
+                [jnp.where(upper, lhs, 0.0), jnp.where(upper, 0.0, lhs)], axis=1
+            ).astype(BF16)
             acc = jnp.zeros((GROUP, depth), F32)
-            for j in range(GROUP):
-                acc = jnp.where(sub == j, dot(lhs, held[start + j]), acc)
+            for q in range(GROUP // 4):
+                four = [held[start + 4 * q + i] for i in range(4)]
+                rhs = jnp.concatenate(
+                    [
+                        jnp.concatenate(four[:2], axis=1),
+                        jnp.concatenate(four[2:], axis=1),
+                    ],
+                    axis=0,
+                )
+                both = dot(lhs, rhs)
+                acc = jnp.where(quad == q, jnp.where(even, both[:, :depth], both[:, depth:]), acc)
             prod[pl.ds(start, GROUP), :] = acc
 
         return exact_dot(to_col, prod[...])
@@ -210,25 +246,18 @@
     def forward(field):
         hi = field.astype(BF16)
         lo = (field - hi.astype(F32)).astype(BF16)
-        pick[0] = dot(from_col, hi).astype(BF16)
-        pick[1] = dot(from_col, lo).astype(BF16)
-        sub = lax.broadcasted_iota(jnp.int32, (2 * GROUP, width), 0) & (GROUP - 1)
-
-        @pl.loop(0, groups)
-        def _(g):
-            start = pl.multiple_of(g * GROUP, GROUP)
-            lhs = jnp.concatenate(
-                [pick[0, pl.ds(start, GROUP), :], pick[1, pl.ds(start, GROUP), :]], axis=0
-            )
-            acc = jnp.zeros((2 * GROUP, width), F32)
+        rhs = jnp.concatenate([dot(from_col, hi).T, dot(from_col, lo).T], axis=1).astype(BF16)
+        lane = lax.broadcasted_iota(jnp.int32, (width, slots), 1)
+
+        def step(g, acc):
             for j in range(GROUP):
-                one = lax.dot_general(
-                    lhs, held[start + j], (((1,), (1,)), ((), ())), preferred_element_type=F32
-                )
-                acc = jnp.where(sub == j, one, acc)
-            prod[pl.ds(start, GROUP), :] = acc[:GROUP] + acc[GROUP:]
-
-        return exact_dot(to_row, prod[...])
+                slot = g * GROUP + j
+                both = dot(held[slot], rhs)
+                acc = jnp.where(lane == slot, both[:, :slots] + both[:, slots:], acc)
+            return acc
+
+        acc = lax.fori_loop(0, groups, step, jnp.zeros((width, slots), F32))
+        return exact_dot(to_row, acc.T)
 
     def spread_z(s, z, squares):
         for p in range(n_ray):
@@ -417,11 +446,15 @@
             jax.ShapeDtypeStruct((cells, depth), F32),
             jax.ShapeDtypeStruct((share, width), F32),
         ),
-        in_specs=[vmem, pl.BlockSpec(memory_space=pl.ANY), vmem, vmem, vmem, vmem],
+        in_specs=[pl.BlockSpec(memory_space=pltpu.HBM)] * 6,
         out_specs=(vmem, vmem),
         scratch_shapes=[
+            pltpu.VMEM((1, slots), jnp.int32),
+            pltpu.VMEM((1, slots), jnp.int32),
+            pltpu.VMEM((1, 1), jnp.int32),
+            pltpu.VMEM((cells, depth), F32),
             pltpu.VMEM((slots, width, depth), BF16),
-            pltpu.VMEM((2, slots, depth), BF16),
+            pltpu.VMEM((slots, depth), BF16),
             pltpu.VMEM((slots, depth), F32),
             pltpu.VMEM((row_blocks, width), F32),
             pltpu.VMEM((2, n_ray, cells + 8, depth), F32),
@@ -435,11 +468,12 @@
             pltpu.VMEM((2, size_y, depth), F32),
             pltpu.VMEM((n_ray, 8, depth), F32),
             pltpu.VMEM((row_blocks, width), F32),
+            dma((5,)),
             dma((slots // GROUP,)),
         ]
         + pairs,
         compiler_params=pltpu.CompilerParams(
-            collective_id=0, has_side_effects=True, vmem_limit_bytes=48 * 2**20
+            collective_id=0, has_side_effects=True, vmem_limit_bytes=64 * 2**20
         ),
     )(
         data.reshape(share, width),

time: 57.9 us -> 54.5 us (0.941)
  local copies, waits for them, and re-layouts: 6.11 us -> 2.62 us
    unnamed x12 -> x2, local copies, waits for them, and re-layouts: 6.11 us -> 2.62 us
where the time goes in v2:
time: 54.5 us; the launch traced here: 54.2 us
  Pallas kernels  50.3 us (92%)
  local copies, waits for them, and re-layouts  2.62 us (5%)
  between operations  1.29 us (2%)
    pallas_call x1, Pallas kernels, shards(): pl.pallas_call(functools.partial(kernel, n_ray, n_tile, size_x, size_y),...  50.3 us
    unnamed x2, local copies, waits for them, and re-layouts  2.62 us

profile of v2, /device:TPU:0, one launch (start us, length us, event | category | flops | bytes accessed | tf_op | source)
XLA Modules:
  0.0 54.2 jit_solution(8934286752466888739)
XLA Ops:
  1.3 50.3 %shard_map.77 = (f32[32,128]{1,0:T(8,128)}, f32[16,128]{1,0:T(8,128)}) custom-call(f32[16,128]{1,0:T(8,128)} %bitcast.10, bf16[128,128,128]{2,1,0:T(8,128)(2,1)} %bitcast.7, s32[1,128]{1,0:T(1,128)} %bitcast.12, s32[1,128]{1,0:T(1,128)} %bitcast.13, s32[1,1]{1,0:T(1,128)S(6)} %copy.10.count_hbm, f32[32,128]{1,0:T(8,128)} %bitcast.8), custom_call_target="tpu_custom_call" | custom-call | tf_op jit(solution)/shard_map/pallas_call | solution.py:443
  51.6 1.3 %copy.11 = f32[4,8,128]{2,1,0:T(8,128)} copy(f32[4,8,128]{2,1,0:T(8,128)} %bitcast.9) | data formatting | bytes 32768
  52.9 1.3 %copy.12 = f32[2048]{0:T(1024)} copy(f32[2048]{0:T(1024)} %bitcast.11) | data formatting | bytes 16384

commit v3 on v2

--- a/solution.py
+++ b/solution.py
@@ -10,6 +10,7 @@
 MESH = pl.DeviceIdType.MESH
 EPS = 1e-06
 GROUP = 16
+TILE = 16
 F32 = jnp.float32
 BF16 = jnp.bfloat16
 
@@ -35,6 +36,15 @@
     p2 = rest.astype(BF16)
     p3 = (rest - p2.astype(F32)).astype(BF16)
     return dot(onehot, p1) + dot(onehot, p2) + dot(onehot, p3)
+
+
+def parts_of(row):
+    p1 = row.astype(BF16).astype(F32)
+    p2 = (row - p1).astype(BF16).astype(F32)
+    p3 = row - p1 - p2
+    at = lax.broadcasted_iota(jnp.int32, (TILE, row.shape[1]), 0)
+    tile = jnp.where(at == 0, p1, jnp.where(at == 1, p2, jnp.where(at == 2, p3, 0.0)))
+    return tile.astype(BF16)
 
 
 def laplace(cur, prev, nxt, xlo, xhi, size_y):
@@ -260,9 +270,10 @@
         return exact_dot(to_row, acc.T)
 
     def spread_z(s, z, squares):
+        rows = parts_of(jnp.sum(squares, axis=0, keepdims=True))
         for p in range(n_ray):
-            zbuf[s, p, 0:cells, :] = z[p * cells : (p + 1) * cells]
-            zbuf[s, p, cells : cells + 8, :] = squares
+            zbuf[s, p, 0:cells, :] = z[p * cells : (p + 1) * cells].astype(BF16)
+            zbuf[s, p, cells : cells + TILE, :] = rows
         zrecv[s, me] = zbuf[s, me]
         return [
             send(
@@ -276,9 +287,9 @@
         ]
 
     def summed(ref, count):
-        acc = ref[0]
+        acc = ref[0].astype(F32)
         for i in range(1, count):
-            acc = acc + ref[i]
+            acc = acc + ref[i].astype(F32)
         return acc
 
     own = pl.ds(pl.multiple_of(me * cells, cells), cells)
@@ -343,7 +354,7 @@
             whole = field[...]
             small[2 * s, t] = fold(whole)
             alpha_copies = to_tiles(small.at[2 * s, t], s_send.at[2 * s], s_recv.at[2 * s])
-            yrecv[s, t] = forward(whole)
+            yrecv[s, t] = forward(whole).astype(BF16)
             y_copies = to_tiles(yrecv.at[s, t], e_send.at[s], e_recv.at[s])
             arrived(halo_copies)
             smooth_v = reg * laplace(
@@ -402,7 +413,10 @@
         else:
             arrived(cell_copies)
             last[me] = fold(raw_rays) + summed(small.at[3], n_tile)
+            earlier = list(started)
             copies = to_rays(last.at[me], f_send, f_recv)
+            for copy in earlier:
+                copy.wait_send()
             arrived(copies)
             beta = jnp.sqrt(total(summed(last, n_ray)) + EPS)
             ubuf[...] = raw_rays
@@ -410,8 +424,19 @@
             rho = jnp.sqrt(rhobar * rhobar + beta * beta)
             phi = rhobar / rho * phibar
             model_ref[...] = model + phi / rho * w_dir
-    for copy in started:
+    for copy in copies:
         copy.wait_send()
+
+
+def hand_out(model_in, rays_in, model_out, rays_out, sem):
+    copies = [
+        pltpu.make_async_copy(model_in, model_out, sem.at[0]),
+        pltpu.make_async_copy(rays_in, rays_out, sem.at[1]),
+    ]
+    for copy in copies:
+        copy.start()
+    for copy in copies:
+        copy.wait()
 
 
 def shards(n_ray, n_tile, data, blocks, block_cols, block_rows, block_counts, reg_weight):
@@ -457,11 +482,11 @@
             pltpu.VMEM((slots, depth), BF16),
             pltpu.VMEM((slots, depth), F32),
             pltpu.VMEM((row_blocks, width), F32),
-            pltpu.VMEM((2, n_ray, cells + 8, depth), F32),
-            pltpu.VMEM((2, n_ray, cells + 8, depth), F32),
+            pltpu.VMEM((2, n_ray, cells + TILE, depth), BF16),
+            pltpu.VMEM((2, n_ray, cells + TILE, depth), BF16),
             pltpu.VMEM((2, n_ray * cells, depth), F32),
             pltpu.VMEM((2, 2, size_y, depth), F32),
-            pltpu.VMEM((2, n_tile, row_blocks, width), F32),
+            pltpu.VMEM((2, n_tile, row_blocks, width), BF16),
             pltpu.VMEM((4, n_tile, 8, depth), F32),
             pltpu.VMEM((cells, depth), F32),
             pltpu.VMEM((2, cells, depth), F32),
@@ -483,6 +508,18 @@
         block_counts,
         reg_weight.reshape(cells, depth),
     )
+    hbm = pl.BlockSpec(memory_space=pltpu.HBM)
+    model, rays = pl.pallas_call(
+        hand_out,
+        out_shape=(
+            jax.ShapeDtypeStruct((cells, depth), F32),
+            jax.ShapeDtypeStruct((share, width), F32),
+        ),
+        in_specs=[hbm, hbm],
+        out_specs=(hbm, hbm),
+        scratch_shapes=[dma((2,))],
+        compiler_params=pltpu.CompilerParams(vmem_limit_bytes=64 * 2**20),
+    )(model, rays)
     return model.reshape(size_x, size_y, depth), rays.reshape(-1)
 
 

time: 54.5 us -> 50.9 us (0.934)
  local copies, waits for them, and re-layouts: 2.62 us -> 0 us
  Pallas kernels: 50.3 us -> 49.4 us
    pallas_call x1, Pallas kernels: 50.3 us -> 47.6 us  [shards(): pl.pallas_call(functools.partial(kernel, n_ray, n_tile, size_x, size_y),...]
    unnamed x2 -> x0, local copies, waits for them, and re-layouts: 2.62 us -> none
    pallas_call x0 -> x1, Pallas kernels: none -> 1.87 us  [shards(): pl.pallas_call(hand_out, out_shape=(jax.ShapeDtypeStruct((cells, depth),...]
where the time goes in v3:
time: 50.9 us; the launch traced here: 50.7 us
  Pallas kernels  49.4 us (97%)
  between operations  1.29 us (3%)
    pallas_call x1, Pallas kernels, shards(): pl.pallas_call(functools.partial(kernel, n_ray, n_tile, size_x, size_y),...  47.6 us
    pallas_call x1, Pallas kernels, shards(): pl.pallas_call(hand_out, out_shape=(jax.ShapeDtypeStruct((cells, depth),...  1.87 us

profile of v3, /device:TPU:0, one launch (start us, length us, event | category | flops | bytes accessed | tf_op | source)
XLA Modules:
  0.0 50.7 jit_solution(2904640599950424290)
XLA Ops:
  1.3 47.6 %shard_map.77 = (f32[32,128]{1,0:T(8,128)}, f32[16,128]{1,0:T(8,128)}) custom-call(f32[16,128]{1,0:T(8,128)} %bitcast.9, bf16[128,128,128]{2,1,0:T(8,128)(2,1)} %bitcast.7, s32[1,128]{1,0:T(1,128)} %bitcast.10, s32[1,128]{1,0:T(1,128)} %bitcast.11, s32[1,1]{1,0:T(1,128)S(6)} %copy.8.count_hbm, f32[32,128]{1,0:T(8,128)} %bitcast.8), custom_call_target="tpu_custom_call" | custom-call | tf_op jit(solution)/shard_map/pallas_call | solution.py:468
  48.9 1.9 %shard_map.78 = (f32[32,128]{1,0:T(8,128)}, f32[16,128]{1,0:T(8,128)}) custom-call(f32[32,128]{1,0:T(8,128)} %get-tuple-element.6.model_in, f32[16,128]{1,0:T(8,128)} %get-tuple-element.7.rays_in), custom_call_target="tpu_custom_call" | custom-call | tf_op jit(solution)/shard_map/pallas_call | solution.py:512

commit v4 on v3

--- a/solution.py
+++ b/solution.py
@@ -11,6 +11,8 @@
 EPS = 1e-06
 GROUP = 16
 TILE = 16
+SPAN = 4
+CHUNK = 8
 F32 = jnp.float32
 BF16 = jnp.bfloat16
 
@@ -30,12 +32,10 @@
     return jnp.dot(a, b, preferred_element_type=F32)
 
 
-def exact_dot(onehot, x):
-    p1 = x.astype(BF16)
-    rest = x - p1.astype(F32)
-    p2 = rest.astype(BF16)
-    p3 = (rest - p2.astype(F32)).astype(BF16)
-    return dot(onehot, p1) + dot(onehot, p2) + dot(onehot, p3)
+def halves(x, axis):
+    hi = x.astype(BF16)
+    lo = (x - hi.astype(F32)).astype(BF16)
+    return jnp.concatenate([hi, lo], axis=axis)
 
 
 def parts_of(row):
@@ -213,8 +213,8 @@
     ).astype(F32)
     from_col = to_col.T.astype(BF16)
     from_row = to_row.T.astype(BF16)
-    to_col = to_col.astype(BF16)
-    to_row = to_row.astype(BF16)
+    to_col = jnp.concatenate([to_col, to_col], axis=1).astype(BF16)
+    to_row = jnp.concatenate([to_row, to_row], axis=1).astype(BF16)
     reg = reg_ref[...]
     has_prev = jnp.where(me > 0, 1.0, 0.0).astype(F32)
     has_next = jnp.where(me < n_ray - 1, 1.0, 0.0).astype(F32)
@@ -228,46 +228,48 @@
         even = (sub & 1) == 0
         quad = lax.shift_right_logical(sub, 2)
 
-        @pl.loop(0, groups)
-        def _(g):
-            if first:
-                block_copy(g).wait()
-            start = pl.multiple_of(g * GROUP, GROUP)
-            lhs = pick[pl.ds(start, GROUP), :].astype(F32)
-            lhs = jnp.concatenate(
-                [jnp.where(upper, lhs, 0.0), jnp.where(upper, 0.0, lhs)], axis=1
-            ).astype(BF16)
-            acc = jnp.zeros((GROUP, depth), F32)
-            for q in range(GROUP // 4):
-                four = [held[start + 4 * q + i] for i in range(4)]
-                rhs = jnp.concatenate(
-                    [
-                        jnp.concatenate(four[:2], axis=1),
-                        jnp.concatenate(four[2:], axis=1),
-                    ],
-                    axis=0,
-                )
-                both = dot(lhs, rhs)
-                acc = jnp.where(quad == q, jnp.where(even, both[:, :depth], both[:, depth:]), acc)
-            prod[pl.ds(start, GROUP), :] = acc
-
-        return exact_dot(to_col, prod[...])
+        @pl.loop(0, groups // SPAN)
+        def _(i):
+            for h in range(SPAN):
+                g = i * SPAN + h
+                if first:
+                    block_copy(g).wait()
+                start = pl.multiple_of(g * GROUP, GROUP)
+                lhs = pick[pl.ds(start, GROUP), :].astype(F32)
+                lhs = jnp.concatenate(
+                    [jnp.where(upper, lhs, 0.0), jnp.where(upper, 0.0, lhs)], axis=1
+                ).astype(BF16)
+                acc = jnp.zeros((GROUP, depth), F32)
+                for q in range(GROUP // 4):
+                    four = [held[start + 4 * q + k] for k in range(4)]
+                    rhs = jnp.concatenate(
+                        [
+                            jnp.concatenate(four[:2], axis=1),
+                            jnp.concatenate(four[2:], axis=1),
+                        ],
+                        axis=0,
+                    )
+                    both = dot(lhs, rhs)
+                    one = jnp.where(even, both[:, :depth], both[:, depth:])
+                    acc = jnp.where(quad == q, one, acc)
+                prod[pl.ds(start, GROUP), :] = acc
+
+        return dot(to_col, halves(prod[...], 0))
 
     def forward(field):
-        hi = field.astype(BF16)
-        lo = (field - hi.astype(F32)).astype(BF16)
-        rhs = jnp.concatenate([dot(from_col, hi).T, dot(from_col, lo).T], axis=1).astype(BF16)
+        rhs = dot(from_col, halves(field, 1)).T.astype(BF16)
         lane = lax.broadcasted_iota(jnp.int32, (width, slots), 1)
 
         def step(g, acc):
-            for j in range(GROUP):
-                slot = g * GROUP + j
-                both = dot(held[slot], rhs)
-                acc = jnp.where(lane == slot, both[:, :slots] + both[:, slots:], acc)
+            start = pl.multiple_of(g * CHUNK, CHUNK)
+            lhs = held[pl.ds(start, CHUNK)].reshape(CHUNK * width, depth)
+            out = dot(jnp.concatenate([lhs, lhs], axis=1), rhs)
+            for j in range(CHUNK):
+                acc = jnp.where(lane == start + j, out[j * width : (j + 1) * width], acc)
             return acc
 
-        acc = lax.fori_loop(0, groups, step, jnp.zeros((width, slots), F32))
-        return exact_dot(to_row, acc.T)
+        acc = lax.fori_loop(0, slots // CHUNK, step, jnp.zeros((width, slots), F32))
+        return dot(to_row, halves(acc.T, 0))
 
     def spread_z(s, z, squares):
         rows = parts_of(jnp.sum(squares, axis=0, keepdims=True))

time: 50.9 us -> 52.9 us (1.039)
  Pallas kernels: 49.4 us -> 51.5 us
    pallas_call x1, Pallas kernels: 47.6 us -> 49.6 us  [shards(): pl.pallas_call(functools.partial(kernel, n_ray, n_tile, size_x, size_y),...]
where the time goes in v4:
time: 52.9 us; the launch traced here: 52.7 us
  Pallas kernels  51.5 us (97%)
  between operations  1.29 us (2%)
    pallas_call x1, Pallas kernels, shards(): pl.pallas_call(functools.partial(kernel, n_ray, n_tile, size_x, size_y),...  49.6 us
    pallas_call x1, Pallas kernels, shards(): pl.pallas_call(hand_out, out_shape=(jax.ShapeDtypeStruct((cells, depth),...  1.87 us

profile of v4, /device:TPU:0, one launch (start us, length us, event | category | flops | bytes accessed | tf_op | source)
XLA Modules:
  0.0 52.7 jit_solution(13033202435351651087)
XLA Ops:
  1.3 49.6 %shard_map.77 = (f32[32,128]{1,0:T(8,128)}, f32[16,128]{1,0:T(8,128)}) custom-call(f32[16,128]{1,0:T(8,128)} %bitcast.9, bf16[128,128,128]{2,1,0:T(8,128)(2,1)} %bitcast.7, s32[1,128]{1,0:T(1,128)} %bitcast.10, s32[1,128]{1,0:T(1,128)} %bitcast.11, s32[1,1]{1,0:T(1,128)S(6)} %copy.8.count_hbm, f32[32,128]{1,0:T(8,128)} %bitcast.8), custom_call_target="tpu_custom_call" | custom-call | tf_op jit(solution)/shard_map/pallas_call | solution.py:470
  50.9 1.9 %shard_map.78 = (f32[32,128]{1,0:T(8,128)}, f32[16,128]{1,0:T(8,128)}) custom-call(f32[32,128]{1,0:T(8,128)} %get-tuple-element.6.model_in, f32[16,128]{1,0:T(8,128)} %get-tuple-element.7.rays_in), custom_call_target="tpu_custom_call" | custom-call | tf_op jit(solution)/shard_map/pallas_call | solution.py:514

commit v5 on v4

--- a/solution.py
+++ b/solution.py
@@ -12,7 +12,7 @@
 GROUP = 16
 TILE = 16
 SPAN = 4
-CHUNK = 8
+CHUNK = 4
 F32 = jnp.float32
 BF16 = jnp.bfloat16
 
@@ -257,18 +257,34 @@
         return dot(to_col, halves(prod[...], 0))
 
     def forward(field):
-        rhs = dot(from_col, halves(field, 1)).T.astype(BF16)
+        picked = dot(from_col, halves(field, 1))
         lane = lax.broadcasted_iota(jnp.int32, (width, slots), 1)
-
-        def step(g, acc):
-            start = pl.multiple_of(g * CHUNK, CHUNK)
-            lhs = held[pl.ds(start, CHUNK)].reshape(CHUNK * width, depth)
-            out = dot(jnp.concatenate([lhs, lhs], axis=1), rhs)
-            for j in range(CHUNK):
-                acc = jnp.where(lane == start + j, out[j * width : (j + 1) * width], acc)
+        even = (lane & 1) == 0
+        pair = lax.shift_right_logical(lane, 1)
+        hi = picked[:, :depth].T
+        lo = picked[:, depth:].T
+        top = jnp.concatenate([jnp.where(even, hi, 0.0), jnp.where(even, lo, 0.0)], axis=1)
+        bottom = jnp.concatenate([jnp.where(even, 0.0, hi), jnp.where(even, 0.0, lo)], axis=1)
+        rhs = jnp.concatenate([top, bottom], axis=0).astype(BF16)
+
+        def step(i, acc):
+            for h in range(SPAN):
+                start = (i * SPAN + h) * CHUNK
+                lhs = jnp.concatenate(
+                    [
+                        jnp.concatenate([held[2 * (start + j)], held[2 * (start + j) + 1]], axis=1)
+                        for j in range(CHUNK)
+                    ],
+                    axis=0,
+                )
+                out = dot(lhs, rhs)
+                out = out[:, :slots] + out[:, slots:]
+                for j in range(CHUNK):
+                    acc = jnp.where(pair == start + j, out[j * width : (j + 1) * width], acc)
             return acc
 
-        acc = lax.fori_loop(0, slots // CHUNK, step, jnp.zeros((width, slots), F32))
+        steps = slots // (2 * CHUNK * SPAN)
+        acc = lax.fori_loop(0, steps, step, jnp.zeros((width, slots), F32))
         return dot(to_row, halves(acc.T, 0))
 
     def spread_z(s, z, squares):

time: 52.9 us -> 48.3 us (0.913)
  Pallas kernels: 51.5 us -> 46.9 us
    pallas_call x1, Pallas kernels: 49.6 us -> 45 us  [shards(): pl.pallas_call(functools.partial(kernel, n_ray, n_tile, size_x, size_y),...]
where the time goes in v5:
time: 48.3 us; the launch traced here: 48.2 us
  Pallas kernels  46.9 us (97%)
  between operations  1.29 us (3%)
    pallas_call x1, Pallas kernels, shards(): pl.pallas_call(functools.partial(kernel, n_ray, n_tile, size_x, size_y),...  45 us
    pallas_call x1, Pallas kernels, shards(): pl.pallas_call(hand_out, out_shape=(jax.ShapeDtypeStruct((cells, depth),...  1.87 us

profile of v5, /device:TPU:0, one launch (start us, length us, event | category | flops | bytes accessed | tf_op | source)
XLA Modules:
  0.0 48.2 jit_solution(7539987657235649824)
XLA Ops:
  1.3 45.0 %shard_map.77 = (f32[32,128]{1,0:T(8,128)}, f32[16,128]{1,0:T(8,128)}) custom-call(f32[16,128]{1,0:T(8,128)} %bitcast.9, bf16[128,128,128]{2,1,0:T(8,128)(2,1)} %bitcast.7, s32[1,128]{1,0:T(1,128)} %bitcast.10, s32[1,128]{1,0:T(1,128)} %bitcast.11, s32[1,1]{1,0:T(1,128)S(6)} %copy.8.count_hbm, f32[32,128]{1,0:T(8,128)} %bitcast.8), custom_call_target="tpu_custom_call" | custom-call | tf_op jit(solution)/shard_map/pallas_call | solution.py:486
  46.3 1.9 %shard_map.78 = (f32[32,128]{1,0:T(8,128)}, f32[16,128]{1,0:T(8,128)}) custom-call(f32[32,128]{1,0:T(8,128)} %get-tuple-element.6.model_in, f32[16,128]{1,0:T(8,128)} %get-tuple-element.7.rays_in), custom_call_target="tpu_custom_call" | custom-call | tf_op jit(solution)/shard_map/pallas_call | solution.py:530

commit v6 on v5

--- a/solution.py
+++ b/solution.py
@@ -11,7 +11,7 @@
 EPS = 1e-06
 GROUP = 16
 TILE = 16
-SPAN = 4
+SPAN = 8
 CHUNK = 4
 F32 = jnp.float32
 BF16 = jnp.bfloat16

time: 48.3 us -> 47.7 us (0.988)
  Pallas kernels: 46.9 us -> 46.3 us
    pallas_call x1, Pallas kernels: 45 us -> 44.4 us  [shards(): pl.pallas_call(functools.partial(kernel, n_ray, n_tile, size_x, size_y),...]
where the time goes in v6:
time: 47.7 us; the launch traced here: 47.5 us
  Pallas kernels  46.3 us (97%)
  between operations  1.29 us (3%)
    pallas_call x1, Pallas kernels, shards(): pl.pallas_call(functools.partial(kernel, n_ray, n_tile, size_x, size_y),...  44.4 us
    pallas_call x1, Pallas kernels, shards(): pl.pallas_call(hand_out, out_shape=(jax.ShapeDtypeStruct((cells, depth),...  1.87 us

profile of v6, /device:TPU:0, one launch (start us, length us, event | category | flops | bytes accessed | tf_op | source)
XLA Modules:
  0.0 47.5 jit_solution(1001800749108200886)
XLA Ops:
  1.3 44.4 %shard_map.77 = (f32[32,128]{1,0:T(8,128)}, f32[16,128]{1,0:T(8,128)}) custom-call(f32[16,128]{1,0:T(8,128)} %bitcast.9, bf16[128,128,128]{2,1,0:T(8,128)(2,1)} %bitcast.7, s32[1,128]{1,0:T(1,128)} %bitcast.10, s32[1,128]{1,0:T(1,128)} %bitcast.11, s32[1,1]{1,0:T(1,128)S(6)} %copy.8.count_hbm, f32[32,128]{1,0:T(8,128)} %bitcast.8), custom_call_target="tpu_custom_call" | custom-call | tf_op jit(solution)/shard_map/pallas_call | solution.py:486
  45.7 1.9 %shard_map.78 = (f32[32,128]{1,0:T(8,128)}, f32[16,128]{1,0:T(8,128)}) custom-call(f32[32,128]{1,0:T(8,128)} %get-tuple-element.6.model_in, f32[16,128]{1,0:T(8,128)} %get-tuple-element.7.rays_in), custom_call_target="tpu_custom_call" | custom-call | tf_op jit(solution)/shard_map/pallas_call | solution.py:530
